TPU v7x, 128 devices: a whole 4x4x4 slice. The times are simulated.
128 devices in a mesh: member: 4 (over z), space: 32 (over y, x, core).
Axes of the slice: x: 4, y: 4, z: 4, core: 2. Of those that a mesh axis runs over, the one named last changes fastest.
Arguments:
- particles: float32 [32, 2, 800, 800], P('member', None, 'space'), may hold values from -8 to 8
- loglik_grad: float32 [32, 2, 800, 800], P('member', None, 'space'), may hold values from -9.1552734e-05 to 9.1552734e-05
- wave_prev: float32 [32, 2, 800, 800], P('member', None, 'space'), may hold values from -6 to 6
- wave_now: float32 [32, 2, 800, 800], P('member', None, 'space'), may hold values from -6 to 6
- ghosts: float32 [32, 8, 800, 800], P('member', None, 'space'), may hold values from -6 to 6
- src_cell: int32 [32], P('member'), may hold values from 0 to 639999
Outputs:
- new_particles: float32 [32, 2, 800, 800], P('member', None, 'space')
- wave_before: float32 [32, 2, 800, 800], P('member', None, 'space')
- wave_after: float32 [32, 2, 800, 800], P('member', None, 'space')
Inputs may be any that keep to these rules, and one draw needn't show every extreme that they name: `src_cell`: the flat index 800 * x + y of each particle's source cell on depth plane 0.
All inputs are finite; a program needn't handle non-finite values.
Results may differ from a plain program's by a relative error of at most 0.0003.
Values sent between devices are 32-bit elements; how exact they have to be, the bound alone decides.
A program may use at most 128 MiB of HBM per device.

v0:
```python
import math

import jax
import jax.numpy as jnp
from jax import lax
from jax.sharding import PartitionSpec as P

GHOST = 4
STEPS = 4


weights = (-205.0 / 72.0, 8.0 / 5.0, -1.0 / 5.0, 8.0 / 315.0, -1.0 / 560.0)
step_size = 0.25
courant = 0.3


def extended(cells, sides, width):
    for axis, dim in sides:
        count = lax.axis_size(axis)
        ends = count - 1
        head = lax.slice_in_dim(cells, 0, width, axis=dim)
        tail = lax.slice_in_dim(cells, cells.shape[dim] - width, cells.shape[dim], axis=dim)
        cells = jnp.concatenate(
            [
                lax.ppermute(tail, axis, [(i, (i + 1) % count) for i in range(ends)]),
                cells,
                lax.ppermute(head, axis, [((i + 1) % count, i) for i in range(ends)]),
            ],
            axis=dim,
        )
    return cells


def laplace(wide, top, bottom):
    extent = wide.shape[-2] - 8
    center = wide[..., 4 : 4 + extent, :]
    depth = center.shape[-3]
    across = center.shape[-1]
    pad_spec = [(0, 0)] * (center.ndim - 1) + [(4, 4)]
    ypad = jnp.pad(center, pad_spec)
    column = jnp.concatenate([top, center, bottom], axis=-3)
    total = 3.0 * weights[0] * center
    for offset in range(1, 5):
        total = total + weights[offset] * (
            wide[..., 4 + offset : 4 + offset + extent, :]
            + wide[..., 4 - offset : 4 - offset + extent, :]
        )
        total = total + weights[offset] * (
            ypad[..., 4 + offset : 4 + offset + across]
            + ypad[..., 4 - offset : 4 - offset + across]
        )
        total = total + weights[offset] * (
            column[..., 4 + offset : 4 + offset + depth, :, :]
            + column[..., 4 - offset : 4 - offset + depth, :, :]
        )
    return total


def source_field(src_cell, first_x, extent, depth, across):
    src_x = src_cell // across
    src_y = src_cell % across
    global_x = first_x + jnp.arange(extent, dtype=jnp.int32)
    ys = jnp.arange(across, dtype=jnp.int32)
    spot = (
        (global_x[None, :, None] == src_x[:, None, None])
        & (ys[None, None, :] == src_y[:, None, None])
    ).astype(jnp.float32)
    plane = (jnp.arange(depth, dtype=jnp.int32) == 0).astype(jnp.float32)
    return plane[None, :, None, None] * spot[:, None, :, :]


def shards(particles, loglik_grad, wave_prev, wave_now, ghosts, src_cell):
    own = particles.shape[0]
    depth = particles.shape[1]
    width = particles.shape[2]
    across = particles.shape[3]
    members = lax.axis_size("member")
    member_idx = lax.axis_index("member")
    space_idx = lax.axis_index("space")
    count = own * members
    every_x, every_g = (
        lax.all_gather(particles, "member", axis=0, tiled=True),
        lax.all_gather(loglik_grad, "member", axis=0, tiled=True),
    )
    xflat = every_x.reshape(count, -1)
    gflat = every_g.reshape(count, -1)
    first_row = member_idx * own
    gram = jnp.dot(
        xflat, xflat.T, precision=lax.Precision.HIGHEST, preferred_element_type=jnp.float32
    )
    norms = jnp.diagonal(gram)
    partial_dist = norms[:, None] + norms[None, :] - 2.0 * gram
    dist = lax.psum(partial_dist, "space")
    offdiag = 1.0 - jnp.eye(count, dtype=jnp.float32)
    band = jnp.sum(dist * offdiag) / (count * (count - 1) * math.log(count + 1))
    kern_rows = jnp.exp(-lax.dynamic_slice_in_dim(dist, first_row, own, 0) / band)
    kernel_grad = jnp.dot(
        kern_rows, gflat, precision=lax.Precision.HIGHEST, preferred_element_type=jnp.float32
    )
    kernel_pos = jnp.dot(
        kern_rows, xflat, precision=lax.Precision.HIGHEST, preferred_element_type=jnp.float32
    )
    mine = particles.reshape(own, -1)
    moved = mine + step_size * (
        0.5 * band * kernel_grad + jnp.sum(kern_rows, axis=1)[:, None] * mine - kernel_pos
    )
    new_particles = moved.reshape(particles.shape)
    coef = jnp.square(courant * (1.0 + 0.3 * jnp.tanh(particles)))
    inject = source_field(src_cell, space_idx * width, width, depth, across)
    top = ghosts[:, :GHOST]
    bottom = ghosts[:, GHOST:]
    prev = wave_prev
    now = wave_now
    for step in range(STEPS):
        wide = extended(now, (("space", 2),), GHOST)
        amplitude = 2.0 * math.cos(1.3 * step)
        following = 2.0 * now - prev + coef * laplace(wide, top, bottom) + amplitude * inject
        prev, now = (now, following)
    return (new_particles, prev, now)


def solution(mesh):
    placed = (
        P("member", None, "space", None),
        P("member", None, "space", None),
        P("member", None, "space", None),
        P("member", None, "space", None),
        P("member", None, "space", None),
        P("member"),
    )
    return jax.shard_map(
        shards,
        mesh=mesh,
        in_specs=placed,
        out_specs=(
            P("member", None, "space", None),
            P("member", None, "space", None),
            P("member", None, "space", None),
        ),
        check_vma=False,
    )
```

profile of v0, /device:TPU:1, one launch (start us, length us, event | category | flops | bytes accessed | tf_op | source)
XLA Modules:
  0.0 337.4 jit_solution(5615601369054783102)
XLA Ops:
  8.0 1.1 fusion.123
  9.1 4.5 %collective-permute-start.1 = (f32[8,2,4,800]{3,1,2,0:T(2,128)S(1)}, f32[8,2,4,800]{3,1,2,0:T(2,128)S(1)}, u32[]{:S(2)}, u32[]{:S(2)}) collective-permute-start(f32[8,2,4,800]{3,1,2,0:T(2,128)S(1)} %get-tuple-element.27), channel_id=1, source_target_pairs={{0,1},{1,2},{2,3},{3,4},{4,5},{5,6},{6,7},{7,8},{8,9},{9,10},{10,1... | collective-permute-start | bytes 614408 | tf_op jit(solution)/shard_map/ppermute | solution.py:25
  13.6 1.9 collective-permute-start
  15.7 7.1 %fusion.119 = (f32[8,4,25,800]{3,1,2,0:T(4,128)S(1)}, f32[8,4,25,800]{3,1,2,0:T(4,128)}) fusion(f32[8,8,25,800]{3,1,2,0:T(8,128)} %param.10), kind=kLoop, calls=%fused_computation.200 | loop fusion | bytes 10240000 | tf_op jit(solution)/shard_map/slice | solution.py:110
  23.1 0.9 constant_dynamic-update-slice_fusion.1
  25.2 19.3 %fusion.57 = (f32[8,2,25,800]{3,1,2,0:T(2,128)S(1)}, f32[8,2,25,800]{3,1,2,0:T(2,128)}, f32[8,2,25,800]{3,1,2,0:T(2,128)}, f32[8,2,25,800]{3,1,2,0:T(2,128)}, f3...) fusion(f32[8,2,25,800]{3,1,2,0:T(2,128)S(1)} %copy-done.13, f32[8,2,25,800]{3,1,2,0:T(2,128)S(1)} %copy-done.7, ...), kind=kLoop, calls=%fused_computation.82 | loop fusion | flops 16000000 | bytes 35200008 | tf_op jit(solution)/shard_map/add | solution.py:117
  44.5 1.1 copy-done.8
  45.7 3.6 %collective-permute-start.3 = (f32[8,2,4,800]{3,1,2,0:T(2,128)S(1)}, f32[8,2,4,800]{3,1,2,0:T(2,128)S(1)}, u32[]{:S(2)}, u32[]{:S(2)}) collective-permute-start(f32[8,2,4,800]{3,1,2,0:T(2,128)S(1)} %get-tuple-element.25), channel_id=1, source_target_pairs={{0,1},{1,2},{2,3},{3,4},{4,5},{5,6},{6,7},{7,8},{8,9},{9,10},{10,1... | collective-permute-start | bytes 614408 | tf_op jit(solution)/shard_map/ppermute | solution.py:25
  49.3 1.9 collective-permute-start.2
  51.2 1.2 copy.18
  52.4 4.6 %collective-permute-done.2 = f32[8,2,4,800]{3,1,2,0:T(2,128)S(1)} collective-permute-done((f32[8,2,4,800]{3,1,2,0:T(2,128)S(1)}, f32[8,2,4,800]{3,1,2,0:T(2,128)S(1)}, u32[]{:S(2)}, u32[]{:S(2)}) %collective-permute-start.2) | collective-permute-done | bytes 204832 | tf_op jit(solution)/shard_map/ppermute | solution.py:27
  57.1 31.9 %fusion.58 = f32[8,2,25,800]{3,1,2,0:T(2,128)S(1)} fusion(f32[8,2,25,800]{3,1,2,0:T(2,128)} %param.9, f32[8,2,25,800]{3,1,2,0:T(2,128)} %copy-done.8, f32[8,2,25,800]{3,1,2,0:T(2,128)} %get-tuple-element.17, f32[8,2,4,800]{3,1,2,0:T(2,128)S(1)} %collective-permute-done.3, f32[8,2,4,800]{3,1,2,0:T(2,128)S(1)} %collective-permute-done.2, ...), kind=kLoop, calls=%fused_computation.83 | loop fusion | flops 16640000 | bytes 12569608 | tf_op jit(solution)/shard_map/add | solution.py:117
  89.1 1.9 collective-permute-start.5
  91.0 2.4 collective-permute-start.4
  94.0 4.8 %collective-permute-done.4 = f32[8,2,4,800]{3,1,2,0:T(2,128)S(1)} collective-permute-done((f32[8,2,4,800]{3,1,2,0:T(2,128)S(1)}, f32[8,2,4,800]{3,1,2,0:T(2,128)S(1)}, u32[]{:S(2)}, u32[]{:S(2)}) %collective-permute-start.4) | collective-permute-done | bytes 204832 | tf_op jit(solution)/shard_map/ppermute | solution.py:27
  98.8 14.8 %fusion.59 = f32[8,2,25,800]{3,1,2,0:T(2,128)S(1)} fusion(f32[8,2,25,800]{3,1,2,0:T(2,128)S(1)} %copy-done.9, f32[8,2,25,800]{3,1,2,0:T(2,128)S(1)} %fusion.58, f32[8,2,25,800]{3,1,2,0:T(2,128)S(1)} %copy-done.5, f32[8,2,4,800]{3,1,2,0:T(2,128)S(1)} %collective-permute-done.5, f32[8,2,4,800]{3,1,2,0:T(2,128)S(1)} %collective-permute-done.4, ...), kind=kLoop, calls=%fused_computation.84 | loop fusion | flops 16640000 | bytes 12569608 | tf_op jit(solution)/shard_map/add | solution.py:117
  113.7 1.0 copy-done.12
  114.7 1.9 collective-permute-start.7
  116.7 2.6 collective-permute-start.6
  119.3 1.4 copy.17
  120.7 3.3 reshape.86
  124.4 32.7 %fusion.60 = f32[8,2,25,800]{3,1,2,0:T(2,128)} fusion(f32[8,2,25,800]{3,1,2,0:T(2,128)} %copy-done.10, f32[8,2,25,800]{3,1,2,0:T(2,128)} %copy-done.12, f32[8,2,25,800]{3,1,2,0:T(2,128)} %get-tuple-element.17, f32[8,2,4,800]{3,1,2,0:T(2,128)S(1)} %collective-permute-done.7, f32[8,2,4,800]{3,1,2,0:T(2,128)S(1)} %collective-permute-done.6, ...), kind=kLoop, calls=%fused_computation.85 | loop fusion | flops 16640000 | bytes 12569608 | tf_op jit(solution)/shard_map/add | solution.py:117
  157.2 6.6 %copy.19 = f32[32,2,25,800]{3,2,1,0:T(8,128)} copy(f32[32,2,25,800]{3,1,2,0:T(2,128)} %all-gather.5.cloned.1.call-done) | data formatting | bytes 10240000 | tf_op jit(solution)/shard_map/all_gather | solution.py:83
  163.7 7.1 %reshape.87 = f32[32,40000]{1,0:T(8,128)} reshape(f32[32,2,25,800]{3,2,1,0:T(8,128)} %copy.19) | data formatting | bytes 10240000 | tf_op jit(solution)/shard_map/reshape | solution.py:86
  170.8 9.2 %convolution_bitcast_fusion = f32[32,32]{1,0:T(8,128)S(1)} fusion(f32[32,2,25,800]{3,0,2,1:T(8,128)} %all-gather.3.cloned.1.call-done), kind=kOutput, calls=%fused_computation.182 | convolution fusion | flops 491520000 | bytes 5124096 | tf_op jit(solution)/shard_map/dot_general | solution.py:88
  180.8 121.0 %psum.7 = f32[32,32]{1,0:T(8,128)S(1)} all-reduce(f32[32,32]{1,0:T(8,128)S(1)} %multiply_subtract_fusion), channel_id=1, replica_groups=mesh['member'=4,'space'=32] {'space'}, use_global_device_ids=true, to_apply=%region_0.1 | all-reduce | flops 1024 | bytes 8192 | tf_op jit(solution)/shard_map/psum | solution.py:93
  303.7 8.9 %copy.20 = f32[32,2,25,800]{3,2,1,0:T(8,128)} copy(f32[32,2,25,800]{3,0,2,1:T(8,128)} %all-gather.3.cloned.1.call-done) | data formatting | bytes 10240000 | tf_op jit(solution)/shard_map/all_gather | solution.py:82
  312.6 7.2 %reshape.88 = f32[32,40000]{1,0:T(8,128)} reshape(f32[32,2,25,800]{3,2,1,0:T(8,128)} %copy.20) | data formatting | bytes 10240000 | tf_op jit(solution)/shard_map/reshape | solution.py:85
  319.9 4.6 %fusion = f32[8,40000]{1,0:T(8,128)S(1)} fusion(f32[32,40000]{1,0:T(8,128)} %reshape.87, f32[8,40000]{1,0:T(8,128)S(1)} %copy-done.11, f32[8]{0:T(128)S(1)} %fusion.118, f32[]{:T(128)S(6)} %mul_shard_map.3, f32[32,32]{1,0:T(8,128)S(1)} %psum.7, s32[]{:T(128)S(6)} %select_n.19, f32[]{:T(128)S(6)} %div.15), kind=kOutput, calls=%fused_computation.3 | convolution fusion | flops 123840512 | bytes 7686668 | tf_op jit(solution)/shard_map/dot_general | solution.py:97
  324.6 2.5 fusion.2
  327.1 1.3 reshape.89
  328.4 2.2 copy.21
  (61 shorter events, 5.0 us)
Async XLA Ops:
  7.2 8.4 %copy-start.14 = (s32[8]{0:T(128)S(1)}, s32[8]{0:T(128)}, u32[]{:S(2)}) copy-start(s32[8]{0:T(128)} %param.11) | copy-start | bytes 100
  7.2 150.0 %all-gather.5.cloned.1.call-start = ((), (), s32[]{:S(2)}) async-start(), calls=%async_computation.1 | async-start | bytes 7168000 | tf_op jit(solution)/shard_map/all_gather | solution.py:83
  7.9 162.9 %all-gather.3.cloned.1.call-start = ((), (), s32[]{:S(2)}) async-start(), calls=%async_computation | async-start | bytes 7168000 | tf_op jit(solution)/shard_map/all_gather | solution.py:82
  9.1 13.9 %collective-permute-start.1 = (f32[8,2,4,800]{3,1,2,0:T(2,128)S(1)}, f32[8,2,4,800]{3,1,2,0:T(2,128)S(1)}, u32[]{:S(2)}, u32[]{:S(2)}) collective-permute-start(f32[8,2,4,800]{3,1,2,0:T(2,128)S(1)} %get-tuple-element.27), channel_id=1, source_target_pairs={{0,1},{1,2},{2,3},{3,4},{4,5},{5,6},{6,7},{7,8},{8,9},{9,10},{10,1... | collective-permute-start | bytes 614408 | tf_op jit(solution)/shard_map/ppermute | solution.py:25
  13.6 10.4 %collective-permute-start = (f32[8,2,4,800]{3,1,2,0:T(2,128)S(1)}, f32[8,2,4,800]{3,1,2,0:T(2,128)S(1)}, u32[]{:S(2)}, u32[]{:S(2)}) collective-permute-start(f32[8,2,4,800]{3,1,2,0:T(2,128)S(1)} %get-tuple-element.26), channel_id=1, source_target_pairs={{1,0},{2,1},{3,2},{4,3},{5,4},{6,5},{7,6},{8,7},{9,8},{10,9},{11,1... | collective-permute-start | bytes 614408 | tf_op jit(solution)/shard_map/ppermute | solution.py:27
  15.7 8.4 %slice-start = ((s8[5734400]{0:T(1024)(128)(4,1)}), s8[4194304]{0:T(1024)(128)(4,1)S(1)}, s32[]{:S(2)}) async-start(s8[5734400]{0:T(1024)(128)(4,1)} %bitcast.10), calls=%async_computation.2 | async-start | bytes 8388608
  15.7 7.3 %copy-start.7 = (f32[8,2,25,800]{3,1,2,0:T(2,128)S(1)}, f32[8,2,25,800]{3,1,2,0:T(2,128)}, u32[]{:S(2)}) copy-start(f32[8,2,25,800]{3,1,2,0:T(2,128)} %param.9) | copy-start | bytes 3840004
  15.7 8.3 %slice-start.1 = ((s8[5734400]{0:T(1024)(128)(4,1)}), s8[1540096]{0:T(1024)(128)(4,1)S(1)}, s32[]{:S(2)}) async-start(s8[5734400]{0:T(1024)(128)(4,1)} %bitcast.10), calls=%async_computation.3 | async-start | bytes 3080192
  23.1 1.6 copy-start
  23.1 2.1 copy-start.13
  44.5 1.1 copy-start.8
  45.7 6.8 %collective-permute-start.3 = (f32[8,2,4,800]{3,1,2,0:T(2,128)S(1)}, f32[8,2,4,800]{3,1,2,0:T(2,128)S(1)}, u32[]{:S(2)}, u32[]{:S(2)}) collective-permute-start(f32[8,2,4,800]{3,1,2,0:T(2,128)S(1)} %get-tuple-element.25), channel_id=1, source_target_pairs={{0,1},{1,2},{2,3},{3,4},{4,5},{5,6},{6,7},{7,8},{8,9},{9,10},{10,1... | collective-permute-start | bytes 614408 | tf_op jit(solution)/shard_map/ppermute | solution.py:25
  49.3 7.7 %collective-permute-start.2 = (f32[8,2,4,800]{3,1,2,0:T(2,128)S(1)}, f32[8,2,4,800]{3,1,2,0:T(2,128)S(1)}, u32[]{:S(2)}, u32[]{:S(2)}) collective-permute-start(f32[8,2,4,800]{3,1,2,0:T(2,128)S(1)} %get-tuple-element.24), channel_id=1, source_target_pairs={{1,0},{2,1},{3,2},{4,3},{5,4},{6,5},{7,6},{8,7},{9,8},{10,9},{11,1... | collective-permute-start | bytes 614408 | tf_op jit(solution)/shard_map/ppermute | solution.py:27
  57.0 41.7 %copy-start.1 = (f32[8,2,25,800]{3,1,2,0:T(2,128)S(1)}, f32[8,2,25,800]{3,1,2,0:T(2,128)}, u32[]{:S(2)}) copy-start(f32[8,2,25,800]{3,1,2,0:T(2,128)} %get-tuple-element.13) | copy-start | bytes 3840004
  57.0 41.7 %copy-start.2 = (f32[8,2,25,800]{3,1,2,0:T(2,128)S(1)}, f32[8,2,25,800]{3,1,2,0:T(2,128)}, u32[]{:S(2)}) copy-start(f32[8,2,25,800]{3,1,2,0:T(2,128)} %get-tuple-element.14) | copy-start | bytes 3840004
  57.0 41.7 %copy-start.3 = (f32[8,2,25,800]{3,1,2,0:T(2,128)S(1)}, f32[8,2,25,800]{3,1,2,0:T(2,128)}, u32[]{:S(2)}) copy-start(f32[8,2,25,800]{3,1,2,0:T(2,128)} %get-tuple-element.15) | copy-start | bytes 3840004
  57.0 41.7 %copy-start.4 = (f32[8,2,25,800]{3,1,2,0:T(2,128)S(1)}, f32[8,2,25,800]{3,1,2,0:T(2,128)}, u32[]{:S(2)}) copy-start(f32[8,2,25,800]{3,1,2,0:T(2,128)} %get-tuple-element.16) | copy-start | bytes 3840004
  57.0 41.7 %copy-start.5 = (f32[8,2,25,800]{3,1,2,0:T(2,128)S(1)}, f32[8,2,25,800]{3,1,2,0:T(2,128)}, u32[]{:S(2)}) copy-start(f32[8,2,25,800]{3,1,2,0:T(2,128)} %get-tuple-element.17) | copy-start | bytes 3840004
  57.0 41.7 %copy-start.9 = (f32[8,2,25,800]{3,1,2,0:T(2,128)S(1)}, f32[8,2,25,800]{3,1,2,0:T(2,128)}, u32[]{:S(2)}) copy-start(f32[8,2,25,800]{3,1,2,0:T(2,128)} %copy-done.8) | copy-start | bytes 3840004
  89.0 24.6 %copy-start.10 = (f32[8,2,25,800]{3,1,2,0:T(2,128)}, f32[8,2,25,800]{3,1,2,0:T(2,128)S(1)}, u32[]{:S(2)}) copy-start(f32[8,2,25,800]{3,1,2,0:T(2,128)S(1)} %fusion.58) | copy-start | bytes 3840004
  89.1 4.9 %collective-permute-start.5 = (f32[8,2,4,800]{3,1,2,0:T(2,128)S(1)}, f32[8,2,4,800]{3,1,2,0:T(2,128)S(1)}, u32[]{:S(2)}, u32[]{:S(2)}) collective-permute-start(f32[8,2,4,800]{3,1,2,0:T(2,128)S(1)} %get-tuple-element.23), channel_id=1, source_target_pairs={{0,1},{1,2},{2,3},{3,4},{4,5},{5,6},{6,7},{7,8},{8,9},{9,10},{10,1... | collective-permute-start | bytes 614408 | tf_op jit(solution)/shard_map/ppermute | solution.py:25
  91.0 7.7 %collective-permute-start.4 = (f32[8,2,4,800]{3,1,2,0:T(2,128)S(1)}, f32[8,2,4,800]{3,1,2,0:T(2,128)S(1)}, u32[]{:S(2)}, u32[]{:S(2)}) collective-permute-start(f32[8,2,4,800]{3,1,2,0:T(2,128)S(1)} %get-tuple-element.22), channel_id=1, source_target_pairs={{1,0},{2,1},{3,2},{4,3},{5,4},{6,5},{7,6},{8,7},{9,8},{10,9},{11,1... | collective-permute-start | bytes 614408 | tf_op jit(solution)/shard_map/ppermute | solution.py:27
  113.6 1.1 copy-start.12
  114.7 9.3 %collective-permute-start.7 = (f32[8,2,4,800]{3,1,2,0:T(2,128)S(1)}, f32[8,2,4,800]{3,1,2,0:T(2,128)S(1)}, u32[]{:S(2)}, u32[]{:S(2)}) collective-permute-start(f32[8,2,4,800]{3,1,2,0:T(2,128)S(1)} %get-tuple-element.21), channel_id=1, source_target_pairs={{0,1},{1,2},{2,3},{3,4},{4,5},{5,6},{6,7},{7,8},{8,9},{9,10},{10,1... | collective-permute-start | bytes 614408 | tf_op jit(solution)/shard_map/ppermute | solution.py:25
  116.7 7.7 %collective-permute-start.6 = (f32[8,2,4,800]{3,1,2,0:T(2,128)S(1)}, f32[8,2,4,800]{3,1,2,0:T(2,128)S(1)}, u32[]{:S(2)}, u32[]{:S(2)}) collective-permute-start(f32[8,2,4,800]{3,1,2,0:T(2,128)S(1)} %get-tuple-element.20), channel_id=1, source_target_pairs={{1,0},{2,1},{3,2},{4,3},{5,4},{6,5},{7,6},{8,7},{9,8},{10,9},{11,1... | collective-permute-start | bytes 614408 | tf_op jit(solution)/shard_map/ppermute | solution.py:27
  312.6 7.3 %copy-start.11 = (f32[8,40000]{1,0:T(8,128)S(1)}, f32[8,40000]{1,0:T(8,128)}, u32[]{:S(2)}) copy-start(f32[8,40000]{1,0:T(8,128)} %reshape.86) | copy-start | bytes 3840004
  319.9 4.6 %copy-start.6 = (f32[32,40000]{1,0:T(8,128)S(1)}, f32[32,40000]{1,0:T(8,128)}, u32[]{:S(2)}) copy-start(f32[32,40000]{1,0:T(8,128)} %reshape.88) | copy-start | bytes 15360004
Sparse Core Ops, SparseCore 0:
  9.7 64.4 all-gather.4
  76.4 61.6 all-gather.2
where the time goes:
time: 342 us; the launch traced here: 337 us
  blocking collectives  121 us (35%)
  other arithmetic  99.9 us (29%)
  local copies, waits for them, and re-layouts  52.5 us (15%)
  starting transfers between devices  20.9 us (6%)
  matrix products  16.3 us (5%)
  between operations  15.7 us (5%)
  waiting for transfers between devices  11 us (3%)
    psum x1, blocking collectives, shards(): dist = lax.psum(partial_dist, 'space')  121 us
    add x4, other arithmetic, shards(): 2.0 * now - prev + coef * laplace(wide, top, bottom) + amplitude * inject  98.8 us
    ppermute x4, starting transfers between devices, extended(): lax.ppermute(tail, axis, [(i, (i + 1) % count) for i in range(ends)])  12 us
    ppermute x4, waiting for transfers between devices, extended(): lax.ppermute(head, axis, [((i + 1) % count, i) for i in range(ends)])  9.78 us
    dot_general x1, matrix products, shards(): jnp.dot(xflat, xflat.T, precision=lax.Precision.HIGHEST, preferred_elemen...  9.16 us
    unnamed x39, local copies, waits for them, and re-layouts  9.01 us
    all_gather x1, local copies, waits for them, and re-layouts, shards(): lax.all_gather(particles, 'member', axis=0, tiled=True)  8.94 us
    ppermute x4, starting transfers between devices, extended(): lax.ppermute(head, axis, [((i + 1) % count, i) for i in range(ends)])  8.85 us
  transfers between devices with their start and end apart: 10, of which 4 were waited for; matrix products, arithmetic and copies ran while one was open for 38% of the time, Pallas kernels for 0%

commit v1 on v0

v1 whole, which is shorter than its diff:
```python
import functools
import math

import jax
import jax.numpy as jnp
from jax import lax
from jax.experimental import pallas as pl
from jax.experimental.pallas import tpu as pltpu
from jax.sharding import PartitionSpec as P

MESH = pl.DeviceIdType.MESH
F32 = jnp.float32
GHOST = 4
STEPS = 4
MEMBERS = 4
OWN = 8
COUNT = 32
ROWS = 25
NY = 800
WIDE = 896
HALF = 384
TAIL = 768
CHUNKS = 5
CHUNK = ROWS // CHUNKS

weights = (-205.0 / 72.0, 8.0 / 5.0, -1.0 / 5.0, 8.0 / 315.0, -1.0 / 560.0)
step_size = 0.25
courant = 0.3


def tail_rows(half):
    return list(range(13)) if half == 0 else list(range(13, ROWS))


def kernel(
    x_hbm, g_hbm, wp_hbm, wn_hbm, gh_hbm, src_hbm,
    new, before, after,
    src_ref, xv, gv, prev, wave, gh, gz, coef,
    cells, tails, xtail, gtail, out, otail, ntail,
    spot, acc, part, kmat,
    load_sem, src_sem, own_sem, send_sem, recv_sem, hsend_sem, hrecv_sem, rsend_sem, rrecv_sem,
):
    me = lax.axis_index("member")
    sp = lax.axis_index("space")
    spaces = 32
    my_plane = me // 2
    my_lane = pl.multiple_of((me % 2) * HALF, 128)
    right = (sp + 1) % spaces
    left = (sp + spaces - 1) % spaces
    has_left = sp > 0
    has_right = sp < spaces - 1
    group = sp // 8
    place = sp % 8

    def loads(n, src, dst_of):
        return [
            pltpu.make_async_copy(src.at[p], dst_of(p), load_sem.at[n, p])
            for p in range(OWN)
        ]

    load_x = loads(0, x_hbm, lambda p: xv.at[:, :, p, :])
    load_n = loads(1, wn_hbm, lambda p: wave.at[0, pl.ds(GHOST, ROWS), :, p, :])
    load_h = loads(2, gh_hbm, lambda p: gh.at[:, :, p, :])
    load_p = loads(3, wp_hbm, lambda p: prev.at[:, :, p, :])
    load_g = loads(4, g_hbm, lambda p: gv.at[:, :, p, :])
    for group_of in (load_x, load_n, load_h, load_p, load_g):
        for c in group_of:
            c.start()

    load_src = pltpu.make_async_copy(src_hbm, src_ref, src_sem)
    load_src.start()

    barrier = pltpu.get_barrier_semaphore()
    for d in range(1, MEMBERS):
        pl.semaphore_signal(
            barrier, inc=1, device_id={"member": (me + d) % MEMBERS, "space": sp}, device_id_type=MESH
        )
    peers = [group * 8 + (place + d) % 8 for d in range(1, 8)]
    peers += [((group + d) % 4) * 8 + place for d in range(1, 4)]
    peers += [left, right]
    for peer in peers:
        pl.semaphore_signal(barrier, inc=1, device_id={"member": me, "space": peer}, device_id_type=MESH)

    acc[...] = jnp.zeros_like(acc)
    sub = lax.broadcasted_iota(jnp.int32, (OWN, NY), 0)
    lane = lax.broadcasted_iota(jnp.int32, (OWN, NY), 1)
    sx = jnp.full((OWN, NY), -1, jnp.int32)
    sy = jnp.full((OWN, NY), -1, jnp.int32)
    load_src.wait()
    for p in range(OWN):
        flat = src_ref[p]
        row = lax.div(flat, jnp.int32(NY))
        sx = jnp.where(sub == p, row - sp * ROWS, sx)
        sy = jnp.where(sub == p, flat - row * NY, sy)
    spot[...] = jnp.where(lane == sy, sx, -1)

    @pl.when(jnp.logical_not(has_left))
    def _():
        for t in range(STEPS):
            wave[t, 0:GHOST] = jnp.zeros((GHOST, 2, OWN, NY), F32)

    @pl.when(jnp.logical_not(has_right))
    def _():
        for t in range(STEPS):
            wave[t, GHOST + ROWS :] = jnp.zeros((GHOST, 2, OWN, NY), F32)

    pl.semaphore_wait(barrier, 15)

    def exchange(phase, k, d):
        c = (me + d) % MEMBERS
        source, tail = (xv, xtail) if phase == 0 else (gv, gtail)
        at = pl.ds(pl.multiple_of(phase * COUNT + me * OWN, 8), OWN)
        if k == CHUNKS:
            src = tail.at[c]
            dst = tails.at[:, at, :]
        else:
            rows = pl.ds(k * CHUNK, CHUNK)
            src = source.at[rows, c // 2, :, pl.ds(pl.multiple_of((c % 2) * HALF, 128), HALF)]
            dst = cells.at[rows, at, :]
        if d == 0:
            return pltpu.make_async_copy(src, dst, own_sem.at[phase, k])
        return pltpu.make_async_remote_copy(
            src_ref=src,
            dst_ref=dst,
            send_sem=send_sem.at[phase, k, c],
            recv_sem=recv_sem.at[phase, k, me],
            device_id={"member": c, "space": sp},
            device_id_type=MESH,
        )

    def arrived(phase, k):
        for d in range(1, MEMBERS):
            c = (me + d) % MEMBERS
            at = pl.ds(pl.multiple_of(phase * COUNT + c * OWN, 8), OWN)
            if k == CHUNKS:
                dst = tails.at[:, at, :]
            else:
                dst = cells.at[pl.ds(k * CHUNK, CHUNK), at, :]
            pltpu.make_async_remote_copy(
                src_ref=dst,
                dst_ref=dst,
                send_sem=send_sem.at[phase, k, c],
                recv_sem=recv_sem.at[phase, k, c],
                device_id={"member": c, "space": sp},
                device_id_type=MESH,
            ).wait_recv()
        exchange(phase, k, 0).wait()

    def send(phase, k):
        for d in (2, 1, 3, 0):
            exchange(phase, k, d).start()

    def pack(source, tail):
        for c in range(MEMBERS):
            rows = tail_rows(c % 2)
            for j in range(4):
                pieces = []
                for s in range(4 * j, 4 * j + 4):
                    if s < len(rows):
                        pieces.append(source[rows[s], c // 2, :, TAIL:NY])
                    else:
                        pieces.append(jnp.zeros((OWN, NY - TAIL), F32))
                tail[c, j] = jnp.concatenate(pieces, axis=-1)

    for c in load_x:
        c.wait()
    for k in range(CHUNKS):
        send(0, k)
    pack(xv, xtail)
    send(0, CHUNKS)

    def halo(t, side):
        src = wave.at[t, pl.ds(GHOST if side == 0 else ROWS, GHOST)]
        dst = wave.at[t, pl.ds(GHOST + ROWS if side == 0 else 0, GHOST)]
        return pltpu.make_async_remote_copy(
            src_ref=src,
            dst_ref=dst,
            send_sem=hsend_sem.at[t, side],
            recv_sem=hrecv_sem.at[t, side],
            device_id={"member": me, "space": left if side == 0 else right},
            device_id_type=MESH,
        )

    def halo_start(t):
        @pl.when(has_left)
        def _():
            halo(t, 0).start()

        @pl.when(has_right)
        def _():
            halo(t, 1).start()

    def halo_wait(t):
        @pl.when(has_left)
        def _():
            halo(t, 1).wait_recv()

        @pl.when(has_right)
        def _():
            halo(t, 0).wait_recv()

    for c in load_n:
        c.wait()
    halo_start(0)

    for c in load_h:
        c.wait()

    @pl.loop(0, ROWS)
    def _(r):
        for z in range(2):
            total = jnp.zeros((OWN, NY), F32)
            for k in range(1, GHOST + 1):
                if k > z:
                    total = total + weights[k] * gh[r, GHOST - (k - z)]
                if k > 1 - z:
                    total = total + weights[k] * gh[r, GHOST - 1 + (k - (1 - z))]
            gz[r, z] = total
            coef[r, z] = jnp.square(courant * (1.0 + 0.3 * jnp.tanh(xv[r, z])))

    for c in load_p:
        c.wait()

    blank = jnp.zeros((OWN, WIDE - NY), F32)

    def row_step(t, r):
        amplitude = 2.0 * math.cos(1.3 * t)
        for z in range(2):
            center = wave[t, r + GHOST, z]
            wide = jnp.concatenate([center, blank], axis=-1)
            total = (3.0 * weights[0]) * center + gz[r, z] + weights[1] * wave[t, r + GHOST, 1 - z]
            for k in range(1, GHOST + 1):
                pair = wave[t, r + GHOST + k, z] + wave[t, r + GHOST - k, z]
                turned = pltpu.roll(wide, k, 1) + pltpu.roll(wide, WIDE - k, 1)
                total = total + weights[k] * (pair + turned[:, :NY])
            older = prev[r, z] if t == 0 else wave[t - 1, r + GHOST, z]
            following = 2.0 * center - older + coef[r, z] * total
            if z == 0:
                following = following + jnp.where(spot[...] == r, F32(amplitude), F32(0.0))
            if t == STEPS - 1:
                after[r, z] = following
            else:
                wave[t + 1, r + GHOST, z] = following
            if t == STEPS - 2:
                before[r, z] = following

    def edges(t):
        halo_wait(t)

        @pl.loop(0, 2 * GHOST)
        def _(i):
            row_step(t, jnp.where(i < GHOST, i, i + ROWS - 2 * GHOST))

        if t < STEPS - 1:
            halo_start(t + 1)

    def inner(t):
        @pl.loop(GHOST, ROWS - GHOST)
        def _(r):
            row_step(t, r)

    pairs = [(a, a, k) for a in range(MEMBERS) for k in range(1, 5)]
    pairs += [(a, b, k) for a in range(MEMBERS) for b in range(a + 1, MEMBERS) for k in range(8)]

    def add_pairs(load):
        blocks = [load(a) for a in range(MEMBERS)]
        turned = {}
        for n, (a, b, k) in enumerate(pairs):
            if (b, k) not in turned:
                turned[b, k] = blocks[b] if k == 0 else pltpu.roll(blocks[b], OWN - k, 0)
            gap = blocks[a] - turned[b, k]
            gap = gap * gap
            total = gap[:, :128]
            for i in range(1, gap.shape[1] // 128):
                total = total + gap[:, 128 * i : 128 * i + 128]
            acc[n] += total

    def distances(k):
        arrived(0, k)
        if k == CHUNKS:
            @pl.loop(0, 4)
            def _(j):
                add_pairs(lambda a: tails[j, OWN * a : OWN * a + OWN])
        else:
            @pl.loop(k * CHUNK, (k + 1) * CHUNK)
            def _(r):
                add_pairs(lambda a: cells[r, OWN * a : OWN * a + OWN])

    sub8 = lax.broadcasted_iota(jnp.int32, (OWN, 128), 0)
    lane8 = lax.broadcasted_iota(jnp.int32, (OWN, 128), 1)

    def matrix():
        m = jnp.zeros((OWN, 128), F32)
        for n, (a, b, k) in enumerate(pairs):
            v = jnp.broadcast_to(jnp.sum(acc[n], axis=1, keepdims=True), (OWN, 128))
            m = jnp.where(lane8 == COUNT * a + OWN * b + (sub8 + k) % OWN, v, m)
            if a != b or k < 4:
                v = v if k == 0 else pltpu.roll(v, k, 0)
                m = jnp.where(lane8 == COUNT * b + OWN * a + (sub8 + OWN - k) % OWN, v, m)
        return m

    def stage(n):
        if n == 0:
            return MEMBERS, me, lambda d: {"member": (me + d) % MEMBERS, "space": sp}, 0
        if n == 1:
            return 8, place, lambda d: {"member": me, "space": group * 8 + (place + d) % 8}, 4
        return 4, group, lambda d: {"member": me, "space": ((group + d) % 4) * 8 + place}, 12

    def share(n, d):
        size, mine, peer, base = stage(n)
        return pltpu.make_async_remote_copy(
            src_ref=part.at[base + mine],
            dst_ref=part.at[base + mine],
            send_sem=rsend_sem.at[base + d],
            recv_sem=rrecv_sem.at[base + mine],
            device_id=peer(d),
            device_id_type=MESH,
        )

    def reduce_start(n, value):
        size, mine, _, base = stage(n)
        part[base + mine] = value
        for d in range(1, size):
            share(n, d).start()

    def reduce_end(n):
        size, mine, peer, base = stage(n)
        for d in range(1, size):
            slot = base + (mine + d) % size
            pltpu.make_async_remote_copy(
                src_ref=part.at[slot],
                dst_ref=part.at[slot],
                send_sem=rsend_sem.at[base + d],
                recv_sem=rrecv_sem.at[slot],
                device_id=peer(d),
                device_id_type=MESH,
            ).wait_recv()
        total = part[base]
        for i in range(1, size):
            total = total + part[base + i]
        return total

    def mixing(dist):
        band = jnp.sum(dist, keepdims=True) / (COUNT * (COUNT - 1) * math.log(COUNT + 1))
        band = jnp.broadcast_to(band, (OWN, 128))
        kern = jnp.exp(-dist / band)
        for a in range(MEMBERS):
            mine = kern if a == 0 else pltpu.roll(kern, 128 - COUNT * a, 1)
            mine = jnp.where(lane8 < COUNT, mine, 0.0)
            total = jnp.sum(mine, axis=1, keepdims=True)
            on_x = jnp.where(lane8 == OWN * a + sub8, 1.0 + step_size * total, 0.0) - step_size * mine
            on_g = (0.5 * step_size) * band * mine
            both = on_x + pltpu.roll(on_g, COUNT, 1)
            high = both.astype(jnp.bfloat16).astype(F32)
            low = both - high
            kmat[OWN * a : OWN * a + OWN, :128] = high + pltpu.roll(high, 64, 1)
            kmat[OWN * a : OWN * a + OWN, 128:] = low + pltpu.roll(low, 64, 1)

    def mixed(data):
        high = data.astype(jnp.bfloat16)
        low = (data - high.astype(F32)).astype(jnp.bfloat16)
        stack = jnp.concatenate([high, low, high, low], axis=0)
        return jnp.dot(kmat[...].astype(jnp.bfloat16), stack, preferred_element_type=F32)

    def back(k, d):
        c = (me + d) % MEMBERS
        at = pl.ds(pl.multiple_of(c * OWN, 8), OWN)
        if k == CHUNKS:
            src = otail.at[:, at, :]
            dst = ntail.at[me]
        else:
            rows = pl.ds(k * CHUNK, CHUNK)
            src = out.at[rows, at, :]
            dst = new.at[rows, my_plane, :, pl.ds(my_lane, HALF)]
        if d == 0:
            return pltpu.make_async_copy(src, dst, own_sem.at[2, k])
        return pltpu.make_async_remote_copy(
            src_ref=src,
            dst_ref=dst,
            send_sem=send_sem.at[2, k, c],
            recv_sem=recv_sem.at[2, k, me],
            device_id={"member": c, "space": sp},
            device_id_type=MESH,
        )

    def back_arrived(k):
        for d in range(1, MEMBERS):
            c = (me + d) % MEMBERS
            if k == CHUNKS:
                dst = ntail.at[c]
            else:
                lanes = pl.ds(pl.multiple_of((c % 2) * HALF, 128), HALF)
                dst = new.at[pl.ds(k * CHUNK, CHUNK), c // 2, :, lanes]
            pltpu.make_async_remote_copy(
                src_ref=dst,
                dst_ref=dst,
                send_sem=send_sem.at[2, k, c],
                recv_sem=recv_sem.at[2, k, c],
                device_id={"member": c, "space": sp},
                device_id_type=MESH,
            ).wait_recv()
        back(k, 0).wait()

    def update(k):
        arrived(1, k)
        if k == CHUNKS:
            @pl.loop(0, 4)
            def _(j):
                otail[j] = mixed(tails[j])
        else:
            @pl.loop(k * CHUNK, (k + 1) * CHUNK)
            def _(r):
                out[r] = mixed(cells[r])
        for d in (2, 1, 3, 0):
            back(k, d).start()

    edges(0)
    inner(0)
    for c in load_g:
        c.wait()
    pack(gv, gtail)
    distances(0)
    send(1, CHUNKS)
    send(1, 0)
    edges(1)
    distances(1)
    send(1, 1)
    inner(1)
    distances(2)
    send(1, 2)
    distances(3)
    send(1, 3)
    distances(4)
    send(1, 4)
    distances(CHUNKS)
    reduce_start(0, matrix())
    edges(2)
    reduce_start(1, reduce_end(0))
    inner(2)
    reduce_start(2, reduce_end(1))
    edges(3)
    mixing(reduce_end(2))
    update(CHUNKS)
    for k in range(CHUNKS):
        update(k)
    inner(3)

    for k in range(CHUNKS + 1):
        for d in range(1, MEMBERS):
            exchange(0, k, d).wait_send()
            exchange(1, k, d).wait_send()
    back_arrived(CHUNKS)
    for k in range(CHUNKS):
        back_arrived(k)
    for c in range(MEMBERS):
        for s, r in enumerate(tail_rows(c % 2)):
            new[r, c // 2, :, TAIL:NY] = ntail[c, s // 4, :, 32 * (s % 4) : 32 * (s % 4) + 32]

    for k in range(CHUNKS + 1):
        for d in range(1, MEMBERS):
            back(k, d).wait_send()
    for t in range(STEPS):
        @pl.when(has_left)
        def _():
            halo(t, 0).wait_send()

        @pl.when(has_right)
        def _():
            halo(t, 1).wait_send()
    for n in range(3):
        for d in range(1, stage(n)[0]):
            share(n, d).wait_send()


def place_kernel(new, before, after, o_new, o_before, o_after, sem):
    copies = [
        pltpu.make_async_copy(src.at[:, :, p, :], dst.at[p], sem.at[n, p])
        for n, (src, dst) in enumerate(((new, o_new), (before, o_before), (after, o_after)))
        for p in range(OWN)
    ]
    for c in copies:
        c.start()
    for c in copies:
        c.wait()


def shards(particles, loglik_grad, wave_prev, wave_now, ghosts, src_cell):
    keep = lambda a: pltpu.with_memory_space_constraint(a, pltpu.HBM)
    turn = lambda a: a.transpose(0, 2, 1, 3)
    hbm = pl.BlockSpec(memory_space=pltpu.HBM)
    near = pl.BlockSpec(memory_space=pltpu.VMEM)
    vmem = lambda *s: pltpu.VMEM(s, F32)
    inside = jax.ShapeDtypeStruct((ROWS, 2, OWN, NY), F32)
    new, before, after = pl.pallas_call(
        kernel,
        out_shape=(inside,) * 3,
        in_specs=[hbm] * 6,
        out_specs=(near,) * 3,
        scratch_shapes=[
            pltpu.SMEM((OWN,), jnp.int32),
            vmem(ROWS, 2, OWN, NY),
            vmem(ROWS, 2, OWN, NY),
            vmem(ROWS, 2, OWN, NY),
            vmem(STEPS, ROWS + 2 * GHOST, 2, OWN, NY),
            vmem(ROWS, 2 * GHOST, OWN, NY),
            vmem(ROWS, 2, OWN, NY),
            vmem(ROWS, 2, OWN, NY),
            vmem(ROWS, 2 * COUNT, HALF),
            vmem(4, 2 * COUNT, 128),
            vmem(MEMBERS, 4, OWN, 128),
            vmem(MEMBERS, 4, OWN, 128),
            vmem(ROWS, COUNT, HALF),
            vmem(4, COUNT, 128),
            vmem(MEMBERS, 4, OWN, 128),
            pltpu.VMEM((OWN, NY), jnp.int32),
            vmem(64, OWN, 128),
            vmem(16, OWN, 128),
            vmem(COUNT, 256),
            pltpu.SemaphoreType.DMA((5, OWN)),
            pltpu.SemaphoreType.DMA,
            pltpu.SemaphoreType.DMA((3, CHUNKS + 1)),
            pltpu.SemaphoreType.DMA((3, CHUNKS + 1, MEMBERS)),
            pltpu.SemaphoreType.DMA((3, CHUNKS + 1, MEMBERS)),
            pltpu.SemaphoreType.DMA((STEPS, 2)),
            pltpu.SemaphoreType.DMA((STEPS, 2)),
            pltpu.SemaphoreType.DMA((16,)),
            pltpu.SemaphoreType.DMA((16,)),
        ],
        compiler_params=pltpu.CompilerParams(
            collective_id=0, has_side_effects=True, vmem_limit_bytes=48 * 1024 * 1024
        ),
    )(*map(keep, (turn(particles), turn(loglik_grad), turn(wave_prev), turn(wave_now), turn(ghosts), src_cell)))
    placed = jax.ShapeDtypeStruct((OWN, ROWS, 2, NY), F32)
    outs = pl.pallas_call(
        place_kernel,
        out_shape=(placed,) * 3,
        in_specs=[near] * 3,
        out_specs=(hbm,) * 3,
        scratch_shapes=[pltpu.SemaphoreType.DMA((3, OWN))],
        compiler_params=pltpu.CompilerParams(vmem_limit_bytes=4 * 1024 * 1024),
    )(new, before, after)
    return tuple(o.transpose(0, 2, 1, 3) for o in outs)


def solution(mesh):
    split = P("member", None, "space", None)
    return jax.shard_map(
        shards,
        mesh=mesh,
        in_specs=(split,) * 5 + (P("member"),),
        out_specs=(split,) * 3,
        check_vma=False,
    )
```

time: 342 us -> 66.5 us (0.19); the launches traced: 337 us -> 66.2 us
  blocking collectives: 121 us -> 0 us
  other arithmetic: 99.9 us -> 0 us
  Pallas kernels: 0 us -> 65.6 us
  local copies, waits for them, and re-layouts: 52.5 us -> 0 us
  starting transfers between devices: 20.9 us -> 0 us
  matrix products: 16.3 us -> 0 us
  between operations: 15.7 us -> 0.64 us
  waiting for transfers between devices: 11 us -> 0 us
    psum x1 -> x0, blocking collectives: 121 us -> none  [shards(): dist = lax.psum(partial_dist, 'space')]
    add x5 -> x0, other arithmetic: 98.8 us -> none  [the longest x4 98.8 us: shards(): 2.0 * now - prev + coef * laplace(wide, top, bottom) + amplitude * inject]
    pallas_call x0 -> x2, Pallas kernels: none -> 65.6 us  [the longest x1 63.3 us: shards(): pl.pallas_call(kernel, out_shape=(inside,) * 3, in_specs=[hbm] * 6, out_s...]
    ppermute x8 -> x0, starting transfers between devices: 20.8 us -> none  [the longest x4 12 us: extended(): lax.ppermute(tail, axis, [(i, (i + 1) % count) for i in range(ends)])]
    reshape x4 -> x0, local copies, waits for them, and re-layouts: 18.8 us -> none  [the longest x1 7.16 us: shards(): xflat = every_x.reshape(count, -1)]
    dot_general x3 -> x0, matrix products: 16.3 us -> none  [the longest x1 9.16 us: shards(): jnp.dot(xflat, xflat.T, precision=lax.Precision.HIGHEST, preferred_elemen...]
    all_gather x2 -> x0, local copies, waits for them, and re-layouts: 15.5 us -> none  [the longest x1 8.94 us: shards(): lax.all_gather(particles, 'member', axis=0, tiled=True)]
    ppermute x8 -> x0, waiting for transfers between devices: 10.3 us -> none  [the longest x4 9.78 us: extended(): lax.ppermute(head, axis, [((i + 1) % count, i) for i in range(ends)])]
  transfers between devices with their start and end apart: 10 -> 0, of which waited for: 4 -> 0; matrix products, arithmetic and copies ran while one was open for 38% -> 0% of each run, Pallas kernels for 0% -> 0%
where the time goes in v1:
time: 66.5 us; the launch traced here: 66.2 us
  Pallas kernels  65.6 us (99%)
    pallas_call x1, Pallas kernels, shards(): pl.pallas_call(kernel, out_shape=(inside,) * 3, in_specs=[hbm] * 6, out_s...  63.3 us
    pallas_call x1, Pallas kernels, shards(): pl.pallas_call(place_kernel, out_shape=(placed,) * 3, in_specs=[near] * 3...  2.25 us

profile of v1, /device:TPU:1, one launch (start us, length us, event | category | flops | bytes accessed | tf_op | source)
XLA Modules:
  0.0 66.2 jit_solution(10178809456722143141)
XLA Ops:
  0.6 63.3 %shard_map.85 = (f32[25,2,8,800]{3,2,1,0:T(8,128)S(1)}, f32[25,2,8,800]{3,2,1,0:T(8,128)S(1)}, f32[25,2,8,800]{3,2,1,0:T(8,128)S(1)}) custom-call(f32[8,25,2,800]{3,2,1,0:T(2,128)} %bitcast.9, f32[8,25,2,800]{3,2,1,0:T(2,128)} %bitcast.10, f32[8,25,2,800]{3,2,1,0:T(2,128)} %bitcast.11, f32[8,25,2,800]{3,2,1,0:T(2,128)} %bitcast.12, ...), custom_call_target="tpu_custom_call" | custom-call | tf_op jit(solution)/shard_map/pallas_call | solution.py:494
  63.9 2.2 %shard_map.86 = (f32[8,25,2,800]{3,2,1,0:T(2,128)}, f32[8,25,2,800]{3,2,1,0:T(2,128)}, f32[8,25,2,800]{3,2,1,0:T(2,128)}) custom-call(f32[25,2,8,800]{3,2,1,0:T(8,128)S(1)} %get-tuple-element.9.new, f32[25,2,8,800]{3,2,1,0:T(8,128)S(1)} %get-tuple-element.10.before, f32[25,2,8,800]{3,2,1,0:T(8,128)S(1)} %get-tuple-element.11.after), custom_call_target="tpu_custom_call" | custom-call | tf_op jit(solution)/shard_map/pallas_call | solution.py:534

commit v2 on v1

--- a/solution.py
+++ b/solution.py
@@ -63,13 +63,6 @@
     load_h = loads(2, gh_hbm, lambda p: gh.at[:, :, p, :])
     load_p = loads(3, wp_hbm, lambda p: prev.at[:, :, p, :])
     load_g = loads(4, g_hbm, lambda p: gv.at[:, :, p, :])
-    for group_of in (load_x, load_n, load_h, load_p, load_g):
-        for c in group_of:
-            c.start()
-
-    load_src = pltpu.make_async_copy(src_hbm, src_ref, src_sem)
-    load_src.start()
-
     barrier = pltpu.get_barrier_semaphore()
     for d in range(1, MEMBERS):
         pl.semaphore_signal(
@@ -81,29 +74,8 @@
     for peer in peers:
         pl.semaphore_signal(barrier, inc=1, device_id={"member": me, "space": peer}, device_id_type=MESH)
 
-    acc[...] = jnp.zeros_like(acc)
-    sub = lax.broadcasted_iota(jnp.int32, (OWN, NY), 0)
-    lane = lax.broadcasted_iota(jnp.int32, (OWN, NY), 1)
-    sx = jnp.full((OWN, NY), -1, jnp.int32)
-    sy = jnp.full((OWN, NY), -1, jnp.int32)
-    load_src.wait()
-    for p in range(OWN):
-        flat = src_ref[p]
-        row = lax.div(flat, jnp.int32(NY))
-        sx = jnp.where(sub == p, row - sp * ROWS, sx)
-        sy = jnp.where(sub == p, flat - row * NY, sy)
-    spot[...] = jnp.where(lane == sy, sx, -1)
-
-    @pl.when(jnp.logical_not(has_left))
-    def _():
-        for t in range(STEPS):
-            wave[t, 0:GHOST] = jnp.zeros((GHOST, 2, OWN, NY), F32)
-
-    @pl.when(jnp.logical_not(has_right))
-    def _():
-        for t in range(STEPS):
-            wave[t, GHOST + ROWS :] = jnp.zeros((GHOST, 2, OWN, NY), F32)
-
+    for c in load_x + load_n:
+        c.start()
     pl.semaphore_wait(barrier, 15)
 
     def exchange(phase, k, d):
@@ -166,6 +138,10 @@
         c.wait()
     for k in range(CHUNKS):
         send(0, k)
+    load_src = pltpu.make_async_copy(src_hbm, src_ref, src_sem)
+    load_src.start()
+    for c in load_h + load_p + load_g:
+        c.start()
     pack(xv, xtail)
     send(0, CHUNKS)
 
@@ -203,6 +179,29 @@
         c.wait()
     halo_start(0)
 
+    acc[...] = jnp.zeros_like(acc)
+    sub = lax.broadcasted_iota(jnp.int32, (OWN, NY), 0)
+    lane = lax.broadcasted_iota(jnp.int32, (OWN, NY), 1)
+    sx = jnp.full((OWN, NY), -1, jnp.int32)
+    sy = jnp.full((OWN, NY), -1, jnp.int32)
+    load_src.wait()
+    for p in range(OWN):
+        flat = src_ref[p]
+        row = lax.div(flat, jnp.int32(NY))
+        sx = jnp.where(sub == p, row - sp * ROWS, sx)
+        sy = jnp.where(sub == p, flat - row * NY, sy)
+    spot[...] = jnp.where(lane == sy, sx, -1)
+
+    @pl.when(jnp.logical_not(has_left))
+    def _():
+        for t in range(STEPS):
+            wave[t, 0:GHOST] = jnp.zeros((GHOST, 2, OWN, NY), F32)
+
+    @pl.when(jnp.logical_not(has_right))
+    def _():
+        for t in range(STEPS):
+            wave[t, GHOST + ROWS :] = jnp.zeros((GHOST, 2, OWN, NY), F32)
+
     for c in load_h:
         c.wait()
 
@@ -217,9 +216,6 @@
                     total = total + weights[k] * gh[r, GHOST - 1 + (k - (1 - z))]
             gz[r, z] = total
             coef[r, z] = jnp.square(courant * (1.0 + 0.3 * jnp.tanh(xv[r, z])))
-
-    for c in load_p:
-        c.wait()
 
     blank = jnp.zeros((OWN, WIDE - NY), F32)
 
@@ -301,10 +297,10 @@
 
     def stage(n):
         if n == 0:
-            return MEMBERS, me, lambda d: {"member": (me + d) % MEMBERS, "space": sp}, 0
+            return 8, place, lambda d: {"member": me, "space": group * 8 + (place + d) % 8}, 0
         if n == 1:
-            return 8, place, lambda d: {"member": me, "space": group * 8 + (place + d) % 8}, 4
-        return 4, group, lambda d: {"member": me, "space": ((group + d) % 4) * 8 + place}, 12
+            return 4, group, lambda d: {"member": me, "space": ((group + d) % 4) * 8 + place}, 8
+        return MEMBERS, me, lambda d: {"member": (me + d) % MEMBERS, "space": sp}, 12
 
     def share(n, d):
         size, mine, peer, base = stage(n)
@@ -414,35 +410,40 @@
         for d in (2, 1, 3, 0):
             back(k, d).start()
 
+    distances(0)
+    for c in load_p:
+        c.wait()
     edges(0)
     inner(0)
     for c in load_g:
         c.wait()
     pack(gv, gtail)
-    distances(0)
     send(1, CHUNKS)
     send(1, 0)
-    edges(1)
+    send(1, 1)
     distances(1)
-    send(1, 1)
-    inner(1)
     distances(2)
-    send(1, 2)
     distances(3)
-    send(1, 3)
     distances(4)
-    send(1, 4)
     distances(CHUNKS)
     reduce_start(0, matrix())
+    send(1, 2)
+    edges(1)
+    reduce_start(1, reduce_end(0))
+    inner(1)
+    reduce_start(2, reduce_end(1))
+    send(1, 3)
+    send(1, 4)
     edges(2)
-    reduce_start(1, reduce_end(0))
-    inner(2)
-    reduce_start(2, reduce_end(1))
-    edges(3)
     mixing(reduce_end(2))
     update(CHUNKS)
-    for k in range(CHUNKS):
-        update(k)
+    update(0)
+    update(1)
+    update(2)
+    inner(2)
+    update(3)
+    update(4)
+    edges(3)
     inner(3)
 
     for k in range(CHUNKS + 1):
@@ -450,11 +451,11 @@
             exchange(0, k, d).wait_send()
             exchange(1, k, d).wait_send()
     back_arrived(CHUNKS)
-    for k in range(CHUNKS):
-        back_arrived(k)
     for c in range(MEMBERS):
         for s, r in enumerate(tail_rows(c % 2)):
             new[r, c // 2, :, TAIL:NY] = ntail[c, s // 4, :, 32 * (s % 4) : 32 * (s % 4) + 32]
+    for k in range(CHUNKS):
+        back_arrived(k)
 
     for k in range(CHUNKS + 1):
         for d in range(1, MEMBERS):

time: 66.5 us -> 58.2 us (0.88)
  Pallas kernels: 65.6 us -> 57.4 us
    pallas_call x1, Pallas kernels: 63.3 us -> 55.2 us  [shards(): pl.pallas_call(kernel, out_shape=(inside,) * 3, in_specs=[hbm] * 6, out_s...]
where the time goes in v2:
time: 58.2 us; the launch traced here: 58.1 us
  Pallas kernels  57.4 us (99%)
  between operations  0.64 us (1%)
    pallas_call x1, Pallas kernels, shards(): pl.pallas_call(kernel, out_shape=(inside,) * 3, in_specs=[hbm] * 6, out_s...  55.2 us
    pallas_call x1, Pallas kernels, shards(): pl.pallas_call(place_kernel, out_shape=(placed,) * 3, in_specs=[near] * 3...  2.25 us

profile of v2, /device:TPU:1, one launch (start us, length us, event | category | flops | bytes accessed | tf_op | source)
XLA Modules:
  0.0 58.1 jit_solution(15703494766646659034)
XLA Ops:
  0.6 55.2 %shard_map.85 = (f32[25,2,8,800]{3,2,1,0:T(8,128)S(1)}, f32[25,2,8,800]{3,2,1,0:T(8,128)S(1)}, f32[25,2,8,800]{3,2,1,0:T(8,128)S(1)}) custom-call(f32[8,25,2,800]{3,2,1,0:T(2,128)} %bitcast.9, f32[8,25,2,800]{3,2,1,0:T(2,128)} %bitcast.10, f32[8,25,2,800]{3,2,1,0:T(2,128)} %bitcast.11, f32[8,25,2,800]{3,2,1,0:T(2,128)} %bitcast.12, ...), custom_call_target="tpu_custom_call" | custom-call | tf_op jit(solution)/shard_map/pallas_call | solution.py:495
  55.8 2.2 %shard_map.86 = (f32[8,25,2,800]{3,2,1,0:T(2,128)}, f32[8,25,2,800]{3,2,1,0:T(2,128)}, f32[8,25,2,800]{3,2,1,0:T(2,128)}) custom-call(f32[25,2,8,800]{3,2,1,0:T(8,128)S(1)} %get-tuple-element.9.new, f32[25,2,8,800]{3,2,1,0:T(8,128)S(1)} %get-tuple-element.10.before, f32[25,2,8,800]{3,2,1,0:T(8,128)S(1)} %get-tuple-element.11.after), custom_call_target="tpu_custom_call" | custom-call | tf_op jit(solution)/shard_map/pallas_call | solution.py:535

commit v3 on v2

--- a/solution.py
+++ b/solution.py
@@ -418,17 +418,17 @@
     for c in load_g:
         c.wait()
     pack(gv, gtail)
+    distances(1)
+    distances(2)
+    edges(1)
     send(1, CHUNKS)
     send(1, 0)
-    send(1, 1)
-    distances(1)
-    distances(2)
     distances(3)
     distances(4)
     distances(CHUNKS)
+    send(1, 1)
     reduce_start(0, matrix())
     send(1, 2)
-    edges(1)
     reduce_start(1, reduce_end(0))
     inner(1)
     reduce_start(2, reduce_end(1))

time: 58.2 us -> 57.5 us (0.988)
  Pallas kernels: 57.4 us -> 56.7 us
    pallas_call x1, Pallas kernels: 55.2 us -> 54.5 us  [shards(): pl.pallas_call(kernel, out_shape=(inside,) * 3, in_specs=[hbm] * 6, out_s...]
where the time goes in v3:
time: 57.5 us; the launch traced here: 57.4 us
  Pallas kernels  56.7 us (99%)
  between operations  0.64 us (1%)
    pallas_call x1, Pallas kernels, shards(): pl.pallas_call(kernel, out_shape=(inside,) * 3, in_specs=[hbm] * 6, out_s...  54.5 us
    pallas_call x1, Pallas kernels, shards(): pl.pallas_call(place_kernel, out_shape=(placed,) * 3, in_specs=[near] * 3...  2.25 us

profile of v3, /device:TPU:1, one launch (start us, length us, event | category | flops | bytes accessed | tf_op | source)
XLA Modules:
  0.0 57.4 jit_solution(14926045582825363424)
XLA Ops:
  0.6 54.5 %shard_map.85 = (f32[25,2,8,800]{3,2,1,0:T(8,128)S(1)}, f32[25,2,8,800]{3,2,1,0:T(8,128)S(1)}, f32[25,2,8,800]{3,2,1,0:T(8,128)S(1)}) custom-call(f32[8,25,2,800]{3,2,1,0:T(2,128)} %bitcast.9, f32[8,25,2,800]{3,2,1,0:T(2,128)} %bitcast.10, f32[8,25,2,800]{3,2,1,0:T(2,128)} %bitcast.11, f32[8,25,2,800]{3,2,1,0:T(2,128)} %bitcast.12, ...), custom_call_target="tpu_custom_call" | custom-call | tf_op jit(solution)/shard_map/pallas_call | solution.py:495
  55.1 2.2 %shard_map.86 = (f32[8,25,2,800]{3,2,1,0:T(2,128)}, f32[8,25,2,800]{3,2,1,0:T(2,128)}, f32[8,25,2,800]{3,2,1,0:T(2,128)}) custom-call(f32[25,2,8,800]{3,2,1,0:T(8,128)S(1)} %get-tuple-element.9.new, f32[25,2,8,800]{3,2,1,0:T(8,128)S(1)} %get-tuple-element.10.before, f32[25,2,8,800]{3,2,1,0:T(8,128)S(1)} %get-tuple-element.11.after), custom_call_target="tpu_custom_call" | custom-call | tf_op jit(solution)/shard_map/pallas_call | solution.py:535

commit v4 on v3

--- a/solution.py
+++ b/solution.py
@@ -434,10 +434,10 @@
     reduce_start(2, reduce_end(1))
     send(1, 3)
     send(1, 4)
-    edges(2)
     mixing(reduce_end(2))
     update(CHUNKS)
     update(0)
+    edges(2)
     update(1)
     update(2)
     inner(2)

time: 57.5 us -> 57.5 us (level)
  no operation moved by 1% of the time
where the time goes in v4:
time: 57.5 us; the launch traced here: 57.4 us
  Pallas kernels  56.7 us (99%)
  between operations  0.64 us (1%)
    pallas_call x1, Pallas kernels, shards(): pl.pallas_call(kernel, out_shape=(inside,) * 3, in_specs=[hbm] * 6, out_s...  54.5 us
    pallas_call x1, Pallas kernels, shards(): pl.pallas_call(place_kernel, out_shape=(placed,) * 3, in_specs=[near] * 3...  2.25 us

profile of v4, /device:TPU:1, one launch (start us, length us, event | category | flops | bytes accessed | tf_op | source)
XLA Modules:
  0.0 57.4 jit_solution(2098734095614096859)
XLA Ops:
  0.6 54.5 %shard_map.85 = (f32[25,2,8,800]{3,2,1,0:T(8,128)S(1)}, f32[25,2,8,800]{3,2,1,0:T(8,128)S(1)}, f32[25,2,8,800]{3,2,1,0:T(8,128)S(1)}) custom-call(f32[8,25,2,800]{3,2,1,0:T(2,128)} %bitcast.9, f32[8,25,2,800]{3,2,1,0:T(2,128)} %bitcast.10, f32[8,25,2,800]{3,2,1,0:T(2,128)} %bitcast.11, f32[8,25,2,800]{3,2,1,0:T(2,128)} %bitcast.12, ...), custom_call_target="tpu_custom_call" | custom-call | tf_op jit(solution)/shard_map/pallas_call | solution.py:495
  55.1 2.2 %shard_map.86 = (f32[8,25,2,800]{3,2,1,0:T(2,128)}, f32[8,25,2,800]{3,2,1,0:T(2,128)}, f32[8,25,2,800]{3,2,1,0:T(2,128)}) custom-call(f32[25,2,8,800]{3,2,1,0:T(8,128)S(1)} %get-tuple-element.9.new, f32[25,2,8,800]{3,2,1,0:T(8,128)S(1)} %get-tuple-element.10.before, f32[25,2,8,800]{3,2,1,0:T(8,128)S(1)} %get-tuple-element.11.after), custom_call_target="tpu_custom_call" | custom-call | tf_op jit(solution)/shard_map/pallas_call | solution.py:535
